TPU v7x, 32 devices: a whole 2x2x4 slice. The times are simulated.
32 devices in a mesh: seq: 16 (over z, y, x), head: 2 (over core).
Axes of the slice: x: 2, y: 2, z: 4, core: 2. Of those that a mesh axis runs over, the one named last changes fastest.
Arguments:
- query_rows: bfloat16 [16384, 1536], P(('seq', 'head')), may hold values from -150 to 150
- key_rows: bfloat16 [16384, 1536], P(('seq', 'head')), may hold values from -4 to 4
- value_rows: bfloat16 [16384, 1536], P(('seq', 'head')), may hold values from -6 to 6
- out_grad: bfloat16 [16384, 1536], P(('seq', 'head')), may hold values from -180 to 180
- key_blocks: int32 [32, 3], replicated, may hold values from 0 to 31, as said below
- block_counts: int32 [32], replicated, may hold values from 1 to 3
Outputs:
- query_grad: bfloat16 [16384, 1536], P(('seq', 'head'))
- key_grad: bfloat16 [16384, 1536], P(('seq', 'head'))
- value_grad: bfloat16 [16384, 1536], P(('seq', 'head'))
Inputs may be any that keep to these rules, and one draw needn't show every extreme that they name: `key_blocks`: row b lists 3 different key blocks; its first entry is b itself and the others lie within 2 blocks of b.
All inputs are finite; a program needn't handle non-finite values.
Results may differ from a plain program's by a relative error of at most 0.0051.
Values may be sent and summed in bfloat16 or wider, within the bound.
No kernel may reach another device: no remote copies, remote signals or barrier semaphores. Data moves between devices by JAX's collectives and lax.ppermute only.
A program may use at most 192 MiB of HBM per device.

v0:
```python
import functools
import math

import jax
import jax.numpy as jnp
from jax import lax
from jax.experimental import pallas as pl
from jax.experimental.pallas import tpu as pltpu
from jax.sharding import PartitionSpec as P

HEADS = 12
HEAD_DIM = 128
BLOCK = 512
MAXK = 3
GROUP = 4
SHARE = HEADS // GROUP
OWN = GROUP + 2
SEEN = OWN + GROUP + 1
CORES = 2
MEMBERS = GROUP * CORES
SCALE = HEAD_DIM ** -0.5
LOG_SCALE = SCALE * math.log2(math.e)
COST_FLOPS, COST_BYTES = 3.45e+09, 9.00e+06
VMEM_LIMIT = 60 * 1024 * 1024

ANYWHERE = pl.BlockSpec(memory_space=pl.ANY)
SCALARS = pl.BlockSpec(memory_space=pltpu.SMEM)
FAST = pl.BlockSpec(memory_space=pltpu.VMEM)


def pair_rows(left, right):
    return lax.dot_general(
        left, right, (((1,), (1,)), ((), ())), preferred_element_type=jnp.float32
    )


def product(left, right):
    return jnp.dot(left, right, preferred_element_type=jnp.float32)


def copy_all(copies, sem):
    started = [
        pltpu.make_async_copy(source, target, sem.at[at])
        for at, (source, target) in enumerate(copies)
    ]
    for copy in started:
        copy.start()
    for copy in started:
        copy.wait()


def head_columns(head):
    return pl.ds(head * HEAD_DIM, HEAD_DIM)


def cost(microseconds):
    return pl.CostEstimate(
        flops=int(microseconds * COST_FLOPS),
        bytes_accessed=int(microseconds * COST_BYTES),
        transcendentals=0,
    )


def pack_split_kernel(place, key_rows, value_rows, query_rows, out_grad, *refs):
    outs, sem = refs[:-1], refs[-1]
    here = place[0] & (GROUP - 1)
    copies = []
    for away, out in enumerate(outs):
        start = (SHARE * (here ^ away) + CORES) * HEAD_DIM
        columns = pl.ds(pl.multiple_of(start, HEAD_DIM), HEAD_DIM)
        for index, source in enumerate((key_rows, value_rows, query_rows, out_grad)):
            copies.append((source.at[:, columns], out.at[index]))
    copy_all(copies, sem)


def pack_split(place, sources):
    out = jax.ShapeDtypeStruct((len(sources), BLOCK, HEAD_DIM), jnp.bfloat16)
    return pl.pallas_call(
        pack_split_kernel,
        out_shape=[out] * GROUP,
        in_specs=[SCALARS] + [ANYWHERE] * len(sources),
        out_specs=[FAST] * GROUP,
        scratch_shapes=[pltpu.SemaphoreType.DMA((GROUP * len(sources),))],
        compiler_params=pltpu.CompilerParams(vmem_limit_bytes=VMEM_LIMIT),
        cost_estimate=cost(4),
        name="pack_split",
    )(place, *sources)


def pack_kernel(heads, *refs):
    sources, outs, sem = refs[:4], refs[4:6], refs[6]
    copies = []
    for at, head in enumerate(heads):
        for index, source in enumerate(sources):
            target = outs[index // 2].at[at, index % 2]
            copies.append((source.at[:, pl.ds(head * HEAD_DIM, HEAD_DIM)], target))
    copy_all(copies, sem)


def pack(sources, heads):
    out = jax.ShapeDtypeStruct((len(heads), 2, BLOCK, HEAD_DIM), jnp.bfloat16)
    return pl.pallas_call(
        functools.partial(pack_kernel, heads),
        out_shape=[out] * 2,
        in_specs=[ANYWHERE] * 4,
        out_specs=[FAST] * 2,
        scratch_shapes=[pltpu.SemaphoreType.DMA((4 * len(heads),))],
        compiler_params=pltpu.CompilerParams(vmem_limit_bytes=VMEM_LIMIT),
        cost_estimate=cost(6),
        name="pack",
    )(*sources)


def arrange_kernel(waited, place, *refs):
    members = refs[:GROUP]
    ordered, low, high, cross, sem = refs[GROUP + waited :]
    here, core = place[0] & (GROUP - 1), place[1]
    pair = pl.ds(0, 2)
    copies = []
    for away, member in enumerate(members):
        copies.append(pltpu.make_async_copy(member.at[pair], ordered.at[here ^ away], sem.at[away]))
    for copy in copies:
        copy.start()
    for copy in copies:
        copy.wait()
    low[0] = ordered[0]
    high[0] = ordered[GROUP - 1]
    cross[0] = ordered[core * (GROUP - 1)]


def arrange(place, members, after=()):
    block = (2, BLOCK, HEAD_DIM)
    edge = jax.ShapeDtypeStruct((1,) + block, jnp.bfloat16)
    return pl.pallas_call(
        functools.partial(arrange_kernel, len(after)),
        out_shape=[jax.ShapeDtypeStruct((GROUP,) + block, jnp.bfloat16), edge, edge, edge],
        in_specs=[SCALARS] + [ANYWHERE] * (GROUP + len(after)),
        out_specs=[FAST] * 4,
        scratch_shapes=[pltpu.SemaphoreType.DMA((GROUP,))],
        compiler_params=pltpu.CompilerParams(vmem_limit_bytes=16 << 20),
        cost_estimate=cost(2.5),
        name="arrange",
    )(place, *members, *after)


def cut_kernel(pieces, place, member, *refs):
    outs, sem = refs[-1 - len(pieces) : -1], refs[-1]
    copies = []
    for piece, out in zip(pieces, outs):
        start, rows, parts = piece(place[1])
        copies.append((member.at[pl.ds(start, rows), pl.ds(0, parts)], out))
    copy_all(copies, sem)


def cut(place, member, pieces, after=()):
    shapes = [piece(0)[1:] + member.shape[2:] for piece in pieces]
    return pl.pallas_call(
        functools.partial(cut_kernel, pieces),
        out_shape=[jax.ShapeDtypeStruct(shape, member.dtype) for shape in shapes],
        in_specs=[SCALARS] + [ANYWHERE] * (1 + len(after)),
        out_specs=[FAST] * len(pieces),
        scratch_shapes=[pltpu.SemaphoreType.DMA((len(pieces),))],
        compiler_params=pltpu.CompilerParams(vmem_limit_bytes=16 << 20),
        cost_estimate=cost(1.5),
        name="cut",
    )(place, member, *after)


def grads_core(first, place_of, spots, block_of, keys, rows, sums, queries, lists, counts):
    def query_step(spot, carry):
        block = block_of(spot)
        count = counts[block]

        def live(slots):
            query_block, grad_block = rows[spot, 0], rows[spot, 1]
            places = [place_of(lists[block * MAXK + slot] - first) for slot in range(slots)]
            scores = [pair_rows(keys[at, 0], query_block) for at in places]
            peak = functools.reduce(
                jnp.maximum, [jnp.max(member, axis=0, keepdims=True) for member in scores]
            )
            grown = [jnp.exp2(member * LOG_SCALE - peak * LOG_SCALE) for member in scores]
            weight_grads = [pair_rows(keys[at, 1], grad_block) for at in places]
            total = sum(jnp.sum(member, axis=0, keepdims=True) for member in grown)
            share = 1.0 / total
            delta = share * sum(
                jnp.sum(member * other, axis=0, keepdims=True)
                for member, other in zip(grown, weight_grads)
            )
            query_sum = None
            for at, member, other in zip(places, grown, weight_grads):
                weights = member * share
                score_low = (weights * (other - delta)).astype(jnp.bfloat16)
                sums[at, 1] += product(weights.astype(jnp.bfloat16), grad_block)
                sums[at, 0] += product(score_low, query_block) * SCALE
                term = product(keys[at, 0].T, score_low)
                query_sum = term if query_sum is None else query_sum + term
            queries[spot] = (query_sum * SCALE).T.astype(jnp.bfloat16)

        for slots in range(1, MAXK + 1):
            pl.when(count == slots)(functools.partial(live, slots))
        return carry

    lax.fori_loop(0, spots, query_step, 0)


def begin(copies, sem):
    started = [
        pltpu.make_async_copy(source, target, sem.at[at])
        for at, (source, target) in enumerate(copies)
    ]
    for copy in started:
        copy.start()
    return started


def split_grads_kernel(waited, place, lists, counts, *refs):
    member, swapped, below, above, cross = refs[:5]
    rows_in = refs[5 : 5 + GROUP]
    refs = refs[5 + GROUP + waited :]
    query_out, near_out, far_out, low_out, high_out, cross_out = refs[:6]
    keys, rows, sums, queries, rounded, sem = refs[6:]
    chip, core = place[0], place[1]
    first = 2 * (chip & ~(GROUP - 1)) - 2
    here = chip & (GROUP - 1)
    copies = begin(
        [(part.at[pl.ds(2, 2)], rows.at[here ^ away]) for away, part in enumerate(rows_in)]
        + [
            (member, keys.at[pl.ds(1, GROUP)]),
            (swapped, keys.at[pl.ds(OWN, GROUP)]),
            (below.at[0], keys.at[0]),
            (above.at[0], keys.at[OWN - 1]),
            (cross.at[0], keys.at[SEEN - 1]),
        ],
        sem,
    )
    sums[...] = jnp.zeros_like(sums)
    for copy in copies:
        copy.wait()

    def place_of(offset):
        half = offset >> 1
        other = jnp.where((half >= 1) & (half <= GROUP), OWN - 1 + half, SEEN - 1)
        return jnp.where((offset & 1) == core, half, other)

    def block_of(spot):
        return first + 2 + 2 * spot + core

    grads_core(first, place_of, GROUP, block_of, keys, rows, sums, queries, lists, counts)
    copies = begin([(queries, query_out), (sums.at[pl.ds(1, GROUP)], near_out)], sem)
    for index, spot in enumerate((*range(OWN, OWN + GROUP), 0, OWN - 1, SEEN - 1)):
        rounded[index] = sums[spot].astype(jnp.bfloat16)
    more = begin(
        [
            (rounded.at[pl.ds(0, GROUP)], far_out),
            (rounded.at[pl.ds(GROUP, 1)], low_out),
            (rounded.at[pl.ds(GROUP + 1, 1)], high_out),
            (rounded.at[pl.ds(GROUP + 2, 1)], cross_out),
        ],
        sem.at[pl.ds(2, 4)],
    )
    for copy in copies + more:
        copy.wait()


def split_grads(place, lists, counts, member, swapped, edges, rows, after=()):
    block = (BLOCK, HEAD_DIM)
    edge = jax.ShapeDtypeStruct((1, 2) + block, jnp.bfloat16)
    outs = [
        jax.ShapeDtypeStruct((GROUP,) + block, jnp.bfloat16),
        jax.ShapeDtypeStruct((GROUP, 2) + block, jnp.float32),
        jax.ShapeDtypeStruct((GROUP, 2) + block, jnp.bfloat16),
        edge,
        edge,
        edge,
    ]
    return pl.pallas_call(
        functools.partial(split_grads_kernel, len(after)),
        out_shape=outs,
        in_specs=[SCALARS] * 3 + [ANYWHERE] * (5 + GROUP + len(after)),
        out_specs=[ANYWHERE] * len(outs),
        scratch_shapes=[
            pltpu.VMEM((SEEN, 2) + block, jnp.bfloat16),
            pltpu.VMEM((GROUP, 2) + block, jnp.bfloat16),
            pltpu.VMEM((SEEN, 2) + block, jnp.float32),
            pltpu.VMEM((GROUP,) + block, jnp.bfloat16),
            pltpu.VMEM((GROUP + 3, 2) + block, jnp.bfloat16),
            pltpu.SemaphoreType.DMA((GROUP + 5,)),
        ],
        compiler_params=pltpu.CompilerParams(vmem_limit_bytes=VMEM_LIMIT),
        cost_estimate=cost(13),
        name="split_grads",
    )(place, lists, counts, member, swapped, *edges, *rows, *after)


def whole_grads_kernel(waited, place, lists, counts, *refs):
    member, below, above, rows_in = refs[:4]
    refs = refs[4 + waited :]
    query_out, sum_out, edge_out, low_out, high_out = refs[:5]
    keys, rows, sums, queries, rounded, sem = refs[5:]
    first = 2 * (place[0] & ~(GROUP - 1)) - 2
    copies = begin(
        [
            (member, keys.at[pl.ds(2, MEMBERS)]),
            (below, keys.at[pl.ds(0, 2)]),
            (above, keys.at[pl.ds(MEMBERS + 2, 2)]),
            (rows_in, rows),
        ],
        sem,
    )
    sums[...] = jnp.zeros_like(sums)
    for copy in copies:
        copy.wait()
    grads_core(
        first, lambda offset: offset, MEMBERS, lambda spot: first + 2 + spot,
        keys, rows, sums, queries, lists, counts,
    )
    copies = begin(
        [
            (queries, query_out),
            (sums.at[pl.ds(2, 2)], edge_out.at[pl.ds(0, 2)]),
            (sums.at[pl.ds(MEMBERS, 2)], edge_out.at[pl.ds(2, 2)]),
        ],
        sem,
    )
    rounded[...] = sums[...].astype(jnp.bfloat16)
    more = begin(
        [
            (rounded.at[pl.ds(2, MEMBERS)], sum_out),
            (rounded.at[pl.ds(0, 2)], low_out),
            (rounded.at[pl.ds(MEMBERS + 2, 2)], high_out),
        ],
        sem.at[pl.ds(3, 3)],
    )
    for copy in copies + more:
        copy.wait()


def whole_grads(place, lists, counts, member, edges, rows, after=()):
    block = (BLOCK, HEAD_DIM)
    edge = jax.ShapeDtypeStruct((2, 2) + block, jnp.bfloat16)
    outs = [
        jax.ShapeDtypeStruct((MEMBERS,) + block, jnp.bfloat16),
        jax.ShapeDtypeStruct((MEMBERS, 2) + block, jnp.bfloat16),
        jax.ShapeDtypeStruct((4, 2) + block, jnp.float32),
        edge,
        edge,
    ]
    return pl.pallas_call(
        functools.partial(whole_grads_kernel, len(after)),
        out_shape=outs,
        in_specs=[SCALARS] * 3 + [ANYWHERE] * (4 + len(after)),
        out_specs=[ANYWHERE] * len(outs),
        scratch_shapes=[
            pltpu.VMEM((MEMBERS + 4, 2) + block, jnp.bfloat16),
            pltpu.VMEM((MEMBERS, 2) + block, jnp.bfloat16),
            pltpu.VMEM((MEMBERS + 4, 2) + block, jnp.float32),
            pltpu.VMEM((MEMBERS,) + block, jnp.bfloat16),
            pltpu.VMEM((MEMBERS + 4, 2) + block, jnp.bfloat16),
            pltpu.SemaphoreType.DMA((6,)),
        ],
        compiler_params=pltpu.CompilerParams(vmem_limit_bytes=VMEM_LIMIT),
        cost_estimate=cost(22),
        name="whole_grads",
    )(place, lists, counts, member, *edges, rows, *after)


def split_settle_kernel(waited, place, near, far, below, above, cross, queries, *refs):
    outs = refs[waited:]
    here, core = place[0] & (GROUP - 1), place[1]
    for away, out in enumerate(outs):
        spot = here ^ away
        out[:2] = (near[spot] + far[spot].astype(jnp.float32)).astype(jnp.bfloat16)
        out[2] = queries[spot]

        def more(out, spot, *edges):
            total = near[spot] + far[spot].astype(jnp.float32)
            for edge in edges:
                total += edge[0].astype(jnp.float32)
            out[:2] = total.astype(jnp.bfloat16)

        low, high = spot == 0, spot == GROUP - 1
        pl.when(low & (core == 0))(functools.partial(more, out, spot, below, cross))
        pl.when(low & (core == 1))(functools.partial(more, out, spot, below))
        pl.when(high & (core == 0))(functools.partial(more, out, spot, above))
        pl.when(high & (core == 1))(functools.partial(more, out, spot, above, cross))


def split_settle(place, near, far, edges, queries, after=()):
    out = jax.ShapeDtypeStruct((3, BLOCK, HEAD_DIM), jnp.bfloat16)
    return pl.pallas_call(
        functools.partial(split_settle_kernel, len(after)),
        out_shape=[out] * GROUP,
        in_specs=[SCALARS] + [FAST] * 6 + [ANYWHERE] * len(after),
        out_specs=[FAST] * GROUP,
        compiler_params=pltpu.CompilerParams(vmem_limit_bytes=VMEM_LIMIT),
        cost_estimate=cost(4),
        name="split_settle",
    )(place, near, far, *edges, queries, *after)


def whole_settle_kernel(near, below, above, summed, *refs):
    out = refs[-1]
    at = pl.program_id(0)

    @pl.when(at < 2)
    def _():
        out[...] = (near[...] + below[...].astype(jnp.float32)).astype(jnp.bfloat16)

    @pl.when(at >= 2)
    def _():
        out[...] = (near[...] + above[...].astype(jnp.float32)).astype(jnp.bfloat16)


def whole_settle(near, below, above, summed, after=()):
    one = (1, 2, BLOCK, HEAD_DIM)
    return pl.pallas_call(
        whole_settle_kernel,
        grid=(4,),
        out_shape=jax.ShapeDtypeStruct(summed.shape, summed.dtype),
        in_specs=[
            pl.BlockSpec(one, lambda at: (at, 0, 0, 0)),
            pl.BlockSpec(one, lambda at: (jnp.minimum(at, 1), 0, 0, 0)),
            pl.BlockSpec(one, lambda at: (jnp.maximum(at - 2, 0), 0, 0, 0)),
        ]
        + [ANYWHERE] * (1 + len(after)),
        out_specs=pl.BlockSpec(
            one, lambda at: (jnp.where(at < 2, at, MEMBERS - 4 + at), 0, 0, 0)
        ),
        input_output_aliases={3: 0},
        compiler_params=pltpu.CompilerParams(vmem_limit_bytes=16 << 20),
        cost_estimate=cost(3),
        name="whole_settle",
    )(near, below, above, summed, *after)


def gather_split_kernel(place, *refs):
    pieces, outs, sem = refs[:GROUP], refs[GROUP:-1], refs[-1]
    here = place[0] & (GROUP - 1)
    copies = []
    for away, piece in enumerate(pieces):
        start = (SHARE * (here ^ away) + CORES) * HEAD_DIM
        columns = pl.ds(pl.multiple_of(start, HEAD_DIM), HEAD_DIM)
        for index, out in enumerate(outs):
            copies.append((piece.at[index], out.at[:, columns]))
    copy_all(copies, sem)


def gather_split(place, pieces):
    return pl.pallas_call(
        gather_split_kernel,
        out_shape=[jax.ShapeDtypeStruct((BLOCK, HEADS * HEAD_DIM), jnp.bfloat16)] * 3,
        in_specs=[SCALARS] + [FAST] * GROUP,
        out_specs=[ANYWHERE] * 3,
        scratch_shapes=[pltpu.SemaphoreType.DMA((3 * GROUP,))],
        compiler_params=pltpu.CompilerParams(vmem_limit_bytes=16 << 20),
        cost_estimate=cost(3),
        name="gather_split",
    )(place, *pieces)


def gather_kernel(columns, count, *refs):
    outs, sem = refs[-1 - count : -1], refs[-1]
    copies = []
    for at, head in enumerate(columns):
        for index in range(count):
            copies.append((refs[0].at[at, index], outs[index].at[:, head_columns(head)]))
    copy_all(copies, sem)


def gather(columns, pieces, so_far=()):
    count, kept = pieces.shape[1], len(so_far)
    return pl.pallas_call(
        functools.partial(gather_kernel, columns, count),
        out_shape=[jax.ShapeDtypeStruct((BLOCK, HEADS * HEAD_DIM), jnp.bfloat16)] * count,
        in_specs=[FAST] + [ANYWHERE] * kept,
        out_specs=[ANYWHERE] * count,
        scratch_shapes=[pltpu.SemaphoreType.DMA((count * len(columns),))],
        input_output_aliases={1 + at: at for at in range(kept)},
        compiler_params=pltpu.CompilerParams(vmem_limit_bytes=8 << 20),
        cost_estimate=cost(3),
        name="gather",
    )(pieces, *so_far)


def shards(query_rows, key_rows, value_rows, out_grad, key_blocks, block_counts):
    chips = lax.axis_size("seq")
    chip = lax.axis_index("seq")
    core = lax.axis_index("head")
    place = jnp.stack([chip, core]).astype(jnp.int32)
    lists = key_blocks.reshape(-1)
    wide = [list(range(d, d + MEMBERS)) for d in range(0, CORES * chips, MEMBERS)]
    whole_heads = [SHARE * spot + at for spot in range(GROUP) for at in range(CORES)]

    def across(members):
        return [members[0]] + [
            lax.ppermute(members[away], "seq", [(c, c ^ away) for c in range(chips)])
            for away in range(1, GROUP)
        ]

    def regroup_wide(member):
        return lax.all_to_all(
            member, ("seq", "head"), split_axis=0, concat_axis=0, axis_index_groups=wide, tiled=True
        )

    def swap(member):
        return lax.ppermute(member, "head", [(0, 1), (1, 0)])

    def upward(member):
        return lax.ppermute(member, "seq", [(c, c + GROUP) for c in range(chips - GROUP)])

    def downward(member):
        return lax.ppermute(member, "seq", [(c + GROUP, c) for c in range(chips - GROUP)])

    def crosswise(member):
        pairs = [(2 * c + 1, 2 * (c + GROUP)) for c in range(chips - GROUP)]
        return lax.ppermute(member, ("seq", "head"), pairs + [(b, a) for a, b in pairs])

    sources = (key_rows, value_rows, query_rows, out_grad)
    split = across(pack_split(place, sources))
    keys, rows = pack(sources, whole_heads)
    keys = regroup_wide(keys)
    rows = regroup_wide(rows)
    ordered, low, high, cross = arrange(place, split, [])
    edges = [upward(high), downward(low), crosswise(cross)]
    queries, near, far, low, high, cross = split_grads(
        place, lists, block_counts, ordered, swap(ordered), edges, split, []
    )
    edges, far = [upward(high), downward(low), crosswise(cross)], swap(far)
    low, high = cut(
        place,
        keys,
        [lambda core: (0, 2, 2), lambda core: (MEMBERS - 2, 2, 2)],
        [],
    )
    whole_edges = [upward(high), downward(low)]
    split_done = split_settle(place, near, far, edges, queries, [])
    split_out = across(split_done)
    whole_queries, whole_sums, whole_near, low, high = whole_grads(
        place, lists, block_counts, keys, whole_edges, rows, []
    )
    below, above = upward(high), downward(low)
    whole_queries = regroup_wide(whole_queries)
    whole_sums = whole_settle(whole_near, below, above, whole_sums, [whole_queries])
    whole_out = regroup_wide(whole_sums)
    key_grad, value_grad, query_grad = gather_split(place, split_out)
    (query_grad,) = gather(whole_heads, whole_queries[:, None], (query_grad,))
    key_grad, value_grad = gather(whole_heads, whole_out, (key_grad, value_grad))
    return query_grad, key_grad, value_grad


def solution(mesh):
    rows = P(("seq", "head"), None)
    return jax.shard_map(
        shards,
        mesh=mesh,
        in_specs=(rows, rows, rows, rows, P(), P()),
        out_specs=(rows, rows, rows),
        check_vma=False,
    )
```

profile of v0, /device:TPU:0, one launch (start us, length us, event | category | flops | bytes accessed | tf_op | source)
XLA Modules:
  0.0 174.7 jit_solution(5924226482624751465)
XLA Ops:
  1.3 3.8 %pack_split.1 = (bf16[4,512,128]{2,1,0:T(8,128)(2,1)}, bf16[4,512,128]{2,1,0:T(8,128)(2,1)}, bf16[4,512,128]{2,1,0:T(8,128)(2,1)}, bf16[4,512,128]{2,1,0:T(8,128)(2,1)}) custom-call(s32[2]{0:T(128)} %pad_add_fusion.place, bf16[512,1536]{1,0:T(8,128)(2,1)} %key_rows.1, bf16[512,1536]{1,0:T(8,128)(2,1)} %value_rows.1, bf16[512,1536]{1,0:T(8,128)(2,1)} %query_rows.1, ...), custom_call_target="tpu_custom_call" | custom-call | flops 13799999488 | bytes 36000000 | tf_op jit(solution)/shard_map/pack_split/pallas_call | solution.py:78
  5.1 3.0 %collective-permute-start.2 = (bf16[4,512,128]{2,1,0:T(8,128)(2,1)}, bf16[4,512,128]{2,1,0:T(8,128)(2,1)S(1)}, u32[]{:S(2)}, u32[]{:S(2)}) collective-permute-start(bf16[4,512,128]{2,1,0:T(8,128)(2,1)} %get-tuple-element.41), channel_id=1, source_target_pairs={{0,2},{2,0},{4,6},{6,4},{8,10},{10,8},{12,14},{14,12},{16,18},{18,... | collective-permute-start | bytes 1572872 | tf_op jit(solution)/shard_map/ppermute | solution.py:496
  8.1 1.5 collective-permute-start.3
  9.6 4.7 %pack.1 = (bf16[8,2,512,128]{3,2,1,0:T(8,128)(2,1)}, bf16[8,2,512,128]{3,2,1,0:T(8,128)(2,1)}) custom-call(bf16[512,1536]{1,0:T(8,128)(2,1)} %key_rows.1, bf16[512,1536]{1,0:T(8,128)(2,1)} %value_rows.1, bf16[512,1536]{1,0:T(8,128)(2,1)} %query_rows.1, bf16[512,1536]{1,0:T(8,128)(2,1)} %out_grad.1), custom_call_target="tpu_custom_call" | custom-call | flops 20700000256 | bytes 54000000 | tf_op jit(solution)/shard_map/pack/pallas_call | solution.py:102
  14.3 4.2 %all-to-all-start = ((bf16[8,2,512,128]{3,2,1,0:T(8,128)(2,1)}), bf16[8,2,512,128]{3,2,1,0:T(8,128)(2,1)S(1)}, u32[]{:S(2)}, u32[]{:S(2)}) async-start(bf16[8,2,512,128]{3,2,1,0:T(8,128)(2,1)} %get-tuple-element.35), calls=%async_computation | async-start | bytes 4194304 | tf_op jit(solution)/shard_map/all_to_all | solution.py:501
  18.5 2.6 %collective-permute-done.2.refs_1_.refs_6_ = bf16[4,512,128]{2,1,0:T(8,128)(2,1)S(1)} collective-permute-done((bf16[4,512,128]{2,1,0:T(8,128)(2,1)}, bf16[4,512,128]{2,1,0:T(8,128)(2,1)S(1)}, u32[]{:S(2)}, u32[]{:S(2)}) %collective-permute-start.2) | collective-permute-done | bytes 524320 | tf_op jit(solution)/shard_map/ppermute | solution.py:496
  21.8 11.7 %collective-permute-done.3.refs_2_.refs_7_ = bf16[4,512,128]{2,1,0:T(8,128)(2,1)S(1)} collective-permute-done((bf16[4,512,128]{2,1,0:T(8,128)(2,1)}, bf16[4,512,128]{2,1,0:T(8,128)(2,1)S(1)}, u32[]{:S(2)}, u32[]{:S(2)}) %collective-permute-start.3) | collective-permute-done | bytes 524320 | tf_op jit(solution)/shard_map/ppermute | solution.py:496
  37.5 1.6 arrange.1
  41.3 4.2 %collective-permute-start.6 = (bf16[1,2,512,128]{3,2,1,0:T(8,128)(2,1)}, bf16[1,2,512,128]{3,2,1,0:T(8,128)(2,1)}, u32[]{:S(2)}, u32[]{:S(2)}) collective-permute-start(bf16[1,2,512,128]{3,2,1,0:T(8,128)(2,1)} %copy-done.7), channel_id=1, source_target_pairs={{0,8},{2,10},{4,12},{6,14},{8,16},{10,18},{12,20},{14,22},{16,24},... | collective-permute-start | bytes 786440 | tf_op jit(solution)/shard_map/ppermute | solution.py:509
  46.8 1.4 collective-permute-start.8
  48.2 7.2 %all-to-all-done.member.refs_0_ = bf16[8,2,512,128]{3,2,1,0:T(8,128)(2,1)S(1)} async-done(((bf16[8,2,512,128]{3,2,1,0:T(8,128)(2,1)}), bf16[8,2,512,128]{3,2,1,0:T(8,128)(2,1)S(1)}, u32[]{:S(2)}, u32[]{:S(2)}) %all-to-all-start) | async-done | bytes 2097184 | tf_op jit(solution)/shard_map/all_to_all | solution.py:501
  55.4 4.4 %all-to-all-start.1 = ((bf16[8,2,512,128]{3,2,1,0:T(8,128)(2,1)}), bf16[8,2,512,128]{3,2,1,0:T(8,128)(2,1)}, u32[]{:S(2)}, u32[]{:S(2)}) async-start(bf16[8,2,512,128]{3,2,1,0:T(8,128)(2,1)} %get-tuple-element.38), calls=%async_computation.1 | async-start | bytes 4194304 | tf_op jit(solution)/shard_map/all_to_all | solution.py:501
  59.8 1.4 cut.1
  61.2 3.5 %collective-permute-start = (bf16[2,2,512,128]{3,2,1,0:T(8,128)(2,1)S(1)}, bf16[2,2,512,128]{3,2,1,0:T(8,128)(2,1)S(1)}, u32[]{:S(2)}, u32[]{:S(2)}) collective-permute-start(bf16[2,2,512,128]{3,2,1,0:T(8,128)(2,1)S(1)} %get-tuple-element.36), channel_id=1, source_target_pairs={{0,8},{2,10},{4,12},{6,14},{8,16},{10,18},{12,20},{14,22},{16,24},... | collective-permute-start | bytes 1572872 | tf_op jit(solution)/shard_map/ppermute | solution.py:509
  66.1 13.3 %split_grads.1 = (bf16[4,512,128]{2,1,0:T(8,128)(2,1)}, f32[4,2,512,128]{3,2,1,0:T(8,128)}, bf16[4,2,512,128]{3,2,1,0:T(8,128)(2,1)}, bf16[1,2,512,128]{3,2,1,0:...) custom-call(s32[2]{0:T(128)} %pad_add_fusion.place, s32[96]{0:T(128)} %reshape.9.lists, ...), custom_call_target="tpu_custom_call" | custom-call | flops 44849999872 | bytes 117000000 | tf_op jit(solution)/shard_map/split_grads/pallas_call | solution.py:276
  79.7 5.2 %collective-permute-start.10 = (bf16[1,2,512,128]{3,2,1,0:T(8,128)(2,1)}, bf16[1,2,512,128]{3,2,1,0:T(8,128)(2,1)S(1)}, u32[]{:S(2)}, u32[]{:S(2)}) collective-permute-start(bf16[1,2,512,128]{3,2,1,0:T(8,128)(2,1)} %get-tuple-element.50), channel_id=1, source_target_pairs={{0,8},{2,10},{4,12},{6,14},{8,16},{10,18},{12,20},{14,22},{16,24},... | collective-permute-start | bytes 786440 | tf_op jit(solution)/shard_map/ppermute | solution.py:509
  86.2 1.4 collective-permute-start.12
  88.4 23.0 %whole_grads.1 = (bf16[8,512,128]{2,1,0:T(8,128)(2,1)}, bf16[8,2,512,128]{3,2,1,0:T(8,128)(2,1)}, f32[4,2,512,128]{3,2,1,0:T(8,128)}, bf16[2,2,512,128]{3,2,1,0:T(8,128)(2,1)}, bf16[2,2,512,128]{3,2,1,0:T(8,128)(2,1)}) custom-call(s32[2]{0:T(128)} %pad_add_fusion.place, s32[96]{0:T(128)} %reshape.9.lists, s32[32]{0:T(128)} %counts.3, ...), custom_call_target="tpu_custom_call" | custom-call | flops 75900002304 | bytes 198000000 | tf_op jit(solution)/shard_map/whole_grads/pallas_call | solution.py:348
  111.3 7.0 %all-to-all-start.2 = ((bf16[8,512,128]{2,1,0:T(8,128)(2,1)}), bf16[8,512,128]{2,1,0:T(8,128)(2,1)S(1)}, u32[]{:S(2)}, u32[]{:S(2)}) async-start(bf16[8,512,128]{2,1,0:T(8,128)(2,1)} %get-tuple-element.39), calls=%async_computation.2 | async-start | bytes 2097152 | tf_op jit(solution)/shard_map/all_to_all | solution.py:501
  118.3 1.7 collective-permute-start.16
  122.3 3.8 %split_settle.1 = (bf16[3,512,128]{2,1,0:T(8,128)(2,1)}, bf16[3,512,128]{2,1,0:T(8,128)(2,1)}, bf16[3,512,128]{2,1,0:T(8,128)(2,1)}, bf16[3,512,128]{2,1,0:T(8,128)(2,1)}) custom-call(s32[2]{0:T(128)} %pad_add_fusion.place, f32[4,2,512,128]{3,2,1,0:T(8,128)} %get-tuple-element.48.near, bf16[4,2,512,128]{3,2,1,0:T(8,128)(2,1)} %copy-done.14, ...), custom_call_target="tpu_custom_call" | custom-call | flops 13799999488 | bytes 36000000 | tf_op jit(solution)/shard_map/split_settle/pallas_call | solution.py:390
  126.2 2.0 %collective-permute-start.13 = (bf16[3,512,128]{2,1,0:T(8,128)(2,1)}, bf16[3,512,128]{2,1,0:T(8,128)(2,1)S(1)}, u32[]{:S(2)}, u32[]{:S(2)}) collective-permute-start(bf16[3,512,128]{2,1,0:T(8,128)(2,1)} %get-tuple-element.55), channel_id=1, source_target_pairs={{0,2},{2,0},{4,6},{6,4},{8,10},{10,8},{12,14},{14,12},{16,18},{18,... | collective-permute-start | bytes 1179656 | tf_op jit(solution)/shard_map/ppermute | solution.py:496
  128.2 1.5 collective-permute-start.14
  129.7 2.5 %collective-permute-done.16.below = bf16[2,2,512,128]{3,2,1,0:T(8,128)(2,1)S(1)} collective-permute-done((bf16[2,2,512,128]{3,2,1,0:T(8,128)(2,1)}, bf16[2,2,512,128]{3,2,1,0:T(8,128)(2,1)S(1)}, u32[]{:S(2)}, u32[]{:S(2)}) %collective-permute-start.16) | collective-permute-done | bytes 524320 | tf_op jit(solution)/shard_map/ppermute | solution.py:509
  132.1 6.0 %collective-permute-done.17.above = bf16[2,2,512,128]{3,2,1,0:T(8,128)(2,1)S(1)} collective-permute-done((bf16[2,2,512,128]{3,2,1,0:T(8,128)(2,1)}, bf16[2,2,512,128]{3,2,1,0:T(8,128)(2,1)S(1)}, u32[]{:S(2)}, u32[]{:S(2)}) %collective-permute-start.17) | collective-permute-done | bytes 524320 | tf_op jit(solution)/shard_map/ppermute | solution.py:512
  138.1 1.6 copy-done.10
  139.7 1.6 whole_settle.1
  141.3 4.0 %all-to-all-start.3 = ((bf16[8,2,512,128]{3,2,1,0:T(8,128)(2,1)}), bf16[8,2,512,128]{3,2,1,0:T(8,128)(2,1)S(1)}, u32[]{:S(2)}, u32[]{:S(2)}) async-start(bf16[8,2,512,128]{3,2,1,0:T(8,128)(2,1)} %whole_settle.1), calls=%async_computation.3 | async-start | bytes 4194304 | tf_op jit(solution)/shard_map/all_to_all | solution.py:501
  145.3 5.9 %collective-permute-done.15.refs_3_ = bf16[3,512,128]{2,1,0:T(8,128)(2,1)} collective-permute-done((bf16[3,512,128]{2,1,0:T(8,128)(2,1)}, bf16[3,512,128]{2,1,0:T(8,128)(2,1)}, u32[]{:S(2)}, u32[]{:S(2)}) %collective-permute-start.15) | collective-permute-done | bytes 393248 | tf_op jit(solution)/shard_map/ppermute | solution.py:496
  152.2 2.4 %gather_split.1 = (bf16[512,1536]{1,0:T(8,128)(2,1)}, bf16[512,1536]{1,0:T(8,128)(2,1)}, bf16[512,1536]{1,0:T(8,128)(2,1)}) custom-call(s32[2]{0:T(128)S(1)} %copy-done.9, bf16[3,512,128]{2,1,0:T(8,128)(2,1)S(1)} %copy-done.12, bf16[3,512,128]{2,1,0:T(8,128)(2,1)S(1)} %collective-permute-done.13.refs_1_, ...), custom_call_target="tpu_custom_call" | custom-call | flops 10350000128 | bytes 27000000 | tf_op jit(solution)/shard_map/gather_split/pallas_call | solution.py:449
  155.6 17.5 %all-to-all-done.3.refs_0_ = bf16[8,2,512,128]{3,2,1,0:T(8,128)(2,1)S(1)} async-done(((bf16[8,2,512,128]{3,2,1,0:T(8,128)(2,1)}), bf16[8,2,512,128]{3,2,1,0:T(8,128)(2,1)S(1)}, u32[]{:S(2)}, u32[]{:S(2)}) %all-to-all-start.3) | async-done | bytes 2097184 | tf_op jit(solution)/shard_map/all_to_all | solution.py:501
  173.1 1.4 gather.3
  (62 shorter events, 16.8 us)
Async XLA Ops:
  5.1 16.0 %collective-permute-start.2 = (bf16[4,512,128]{2,1,0:T(8,128)(2,1)}, bf16[4,512,128]{2,1,0:T(8,128)(2,1)S(1)}, u32[]{:S(2)}, u32[]{:S(2)}) collective-permute-start(bf16[4,512,128]{2,1,0:T(8,128)(2,1)} %get-tuple-element.41), channel_id=1, source_target_pairs={{0,2},{2,0},{4,6},{6,4},{8,10},{10,8},{12,14},{14,12},{16,18},{18,... | collective-permute-start | bytes 1572872 | tf_op jit(solution)/shard_map/ppermute | solution.py:496
  8.1 25.4 %collective-permute-start.3 = (bf16[4,512,128]{2,1,0:T(8,128)(2,1)}, bf16[4,512,128]{2,1,0:T(8,128)(2,1)S(1)}, u32[]{:S(2)}, u32[]{:S(2)}) collective-permute-start(bf16[4,512,128]{2,1,0:T(8,128)(2,1)} %get-tuple-element.42), channel_id=1, source_target_pairs={{0,4},{2,6},{4,0},{6,2},{8,12},{10,14},{12,8},{14,10},{16,20},{18,... | collective-permute-start | bytes 1572872 | tf_op jit(solution)/shard_map/ppermute | solution.py:496
  9.6 24.7 %collective-permute-start.4 = (bf16[4,512,128]{2,1,0:T(8,128)(2,1)}, bf16[4,512,128]{2,1,0:T(8,128)(2,1)}, u32[]{:S(2)}, u32[]{:S(2)}) collective-permute-start(bf16[4,512,128]{2,1,0:T(8,128)(2,1)} %get-tuple-element.43), channel_id=1, source_target_pairs={{0,6},{2,4},{4,2},{6,0},{8,14},{10,12},{12,10},{14,8},{16,22},{18,... | collective-permute-start | bytes 1572872 | tf_op jit(solution)/shard_map/ppermute | solution.py:496
  14.3 20.1 %copy-start.8 = (s32[2]{0:T(128)S(1)}, s32[2]{0:T(128)}, u32[]{:S(2)}) copy-start(s32[2]{0:T(128)} %pad_add_fusion.place) | copy-start | bytes 28
  14.3 41.1 %all-to-all-start = ((bf16[8,2,512,128]{3,2,1,0:T(8,128)(2,1)}), bf16[8,2,512,128]{3,2,1,0:T(8,128)(2,1)S(1)}, u32[]{:S(2)}, u32[]{:S(2)}) async-start(bf16[8,2,512,128]{3,2,1,0:T(8,128)(2,1)} %get-tuple-element.35), calls=%async_computation | async-start | bytes 4194304 | tf_op jit(solution)/shard_map/all_to_all | solution.py:501
  34.3 1.0 copy-start.3
  35.4 1.0 copy-start.5
  37.5 3.1 %copy-start.13 = (s32[32,3]{0,1:T(4,128)S(1)}, s32[32,3]{0,1:T(4,128)}, u32[]{:S(2)}) copy-start(s32[32,3]{0,1:T(4,128)} %param.10) | copy-start | bytes 1156
  39.8 15.6 %copy-start.1 = (bf16[4,2,512,128]{3,2,1,0:T(8,128)(2,1)}, bf16[4,2,512,128]{3,2,1,0:T(8,128)(2,1)S(1)}, u32[]{:S(2)}) copy-start(bf16[4,2,512,128]{3,2,1,0:T(8,128)(2,1)S(1)} %get-tuple-element.44.refs_0_) | copy-start | bytes 3145732
  40.5 25.6 %collective-permute-start.5 = (bf16[4,2,512,128]{3,2,1,0:T(8,128)(2,1)S(1)}, bf16[4,2,512,128]{3,2,1,0:T(8,128)(2,1)}, u32[]{:S(2)}, u32[]{:S(2)}) collective-permute-start(bf16[4,2,512,128]{3,2,1,0:T(8,128)(2,1)S(1)} %get-tuple-element.44.refs_0_), channel_id=1, source_target_pairs={{0,1},{1,0},{2,3},{3,2},{4,5},{5,4},{6,7},{7,6},{8,9},{9,8},{10,11... | collective-permute-start | bytes 3145736 | tf_op jit(solution)/shard_map/ppermute | solution.py:506
  41.3 23.4 %collective-permute-start.6 = (bf16[1,2,512,128]{3,2,1,0:T(8,128)(2,1)}, bf16[1,2,512,128]{3,2,1,0:T(8,128)(2,1)}, u32[]{:S(2)}, u32[]{:S(2)}) collective-permute-start(bf16[1,2,512,128]{3,2,1,0:T(8,128)(2,1)} %copy-done.7), channel_id=1, source_target_pairs={{0,8},{2,10},{4,12},{6,14},{8,16},{10,18},{12,20},{14,22},{16,24},... | collective-permute-start | bytes 786440 | tf_op jit(solution)/shard_map/ppermute | solution.py:509
  45.5 20.5 %collective-permute-start.7 = (bf16[1,2,512,128]{3,2,1,0:T(8,128)(2,1)}, bf16[1,2,512,128]{3,2,1,0:T(8,128)(2,1)}, u32[]{:S(2)}, u32[]{:S(2)}) collective-permute-start(bf16[1,2,512,128]{3,2,1,0:T(8,128)(2,1)} %copy-done.6), channel_id=1, source_target_pairs={{8,0},{10,2},{12,4},{14,6},{16,8},{18,10},{20,12},{22,14},{24,16},... | collective-permute-start | bytes 786440 | tf_op jit(solution)/shard_map/ppermute | solution.py:512
  46.8 19.3 %collective-permute-start.8 = (bf16[1,2,512,128]{3,2,1,0:T(8,128)(2,1)S(1)}, bf16[1,2,512,128]{3,2,1,0:T(8,128)(2,1)}, u32[]{:S(2)}, u32[]{:S(2)}) collective-permute-start(bf16[1,2,512,128]{3,2,1,0:T(8,128)(2,1)S(1)} %get-tuple-element.47), channel_id=1, source_target_pairs={{1,8},{3,10},{5,12},{7,14},{9,16},{11,18},{13,20},{15,22},{17,24},... | collective-permute-start | bytes 786440 | tf_op jit(solution)/shard_map/ppermute | solution.py:516
  55.4 4.4 %copy-start = (bf16[8,2,512,128]{3,2,1,0:T(8,128)(2,1)}, bf16[8,2,512,128]{3,2,1,0:T(8,128)(2,1)S(1)}, u32[]{:S(2)}) copy-start(bf16[8,2,512,128]{3,2,1,0:T(8,128)(2,1)S(1)} %all-to-all-done.member.refs_0_) | copy-start | bytes 6291460
  55.4 32.2 %all-to-all-start.1 = ((bf16[8,2,512,128]{3,2,1,0:T(8,128)(2,1)}), bf16[8,2,512,128]{3,2,1,0:T(8,128)(2,1)}, u32[]{:S(2)}, u32[]{:S(2)}) async-start(bf16[8,2,512,128]{3,2,1,0:T(8,128)(2,1)} %get-tuple-element.38), calls=%async_computation.1 | async-start | bytes 4194304 | tf_op jit(solution)/shard_map/all_to_all | solution.py:501
  61.2 25.0 %collective-permute-start = (bf16[2,2,512,128]{3,2,1,0:T(8,128)(2,1)S(1)}, bf16[2,2,512,128]{3,2,1,0:T(8,128)(2,1)S(1)}, u32[]{:S(2)}, u32[]{:S(2)}) collective-permute-start(bf16[2,2,512,128]{3,2,1,0:T(8,128)(2,1)S(1)} %get-tuple-element.36), channel_id=1, source_target_pairs={{0,8},{2,10},{4,12},{6,14},{8,16},{10,18},{12,20},{14,22},{16,24},... | collective-permute-start | bytes 1572872 | tf_op jit(solution)/shard_map/ppermute | solution.py:509
  64.7 22.8 %collective-permute-start.1 = (bf16[2,2,512,128]{3,2,1,0:T(8,128)(2,1)}, bf16[2,2,512,128]{3,2,1,0:T(8,128)(2,1)S(1)}, u32[]{:S(2)}, u32[]{:S(2)}) collective-permute-start(bf16[2,2,512,128]{3,2,1,0:T(8,128)(2,1)} %get-tuple-element.37), channel_id=1, source_target_pairs={{8,0},{10,2},{12,4},{14,6},{16,8},{18,10},{20,12},{22,14},{24,16},... | collective-permute-start | bytes 1572872 | tf_op jit(solution)/shard_map/ppermute | solution.py:512
  79.4 41.9 %collective-permute-start.9 = (bf16[4,2,512,128]{3,2,1,0:T(8,128)(2,1)}, bf16[4,2,512,128]{3,2,1,0:T(8,128)(2,1)S(1)}, u32[]{:S(2)}, u32[]{:S(2)}) collective-permute-start(bf16[4,2,512,128]{3,2,1,0:T(8,128)(2,1)} %get-tuple-element.49), channel_id=1, source_target_pairs={{0,1},{1,0},{2,3},{3,2},{4,5},{5,4},{6,7},{7,6},{8,9},{9,8},{10,11... | collective-permute-start | bytes 3145736 | tf_op jit(solution)/shard_map/ppermute | solution.py:506
  79.7 40.3 %collective-permute-start.10 = (bf16[1,2,512,128]{3,2,1,0:T(8,128)(2,1)}, bf16[1,2,512,128]{3,2,1,0:T(8,128)(2,1)S(1)}, u32[]{:S(2)}, u32[]{:S(2)}) collective-permute-start(bf16[1,2,512,128]{3,2,1,0:T(8,128)(2,1)} %get-tuple-element.50), channel_id=1, source_target_pairs={{0,8},{2,10},{4,12},{6,14},{8,16},{10,18},{12,20},{14,22},{16,24},... | collective-permute-start | bytes 786440 | tf_op jit(solution)/shard_map/ppermute | solution.py:509
  84.9 36.5 %collective-permute-start.11 = (bf16[1,2,512,128]{3,2,1,0:T(8,128)(2,1)}, bf16[1,2,512,128]{3,2,1,0:T(8,128)(2,1)}, u32[]{:S(2)}, u32[]{:S(2)}) collective-permute-start(bf16[1,2,512,128]{3,2,1,0:T(8,128)(2,1)} %get-tuple-element.51), channel_id=1, source_target_pairs={{8,0},{10,2},{12,4},{14,6},{16,8},{18,10},{20,12},{22,14},{24,16},... | collective-permute-start | bytes 786440 | tf_op jit(solution)/shard_map/ppermute | solution.py:512
  86.2 1.4 copy-start.15
  86.2 35.2 %collective-permute-start.12 = (bf16[1,2,512,128]{3,2,1,0:T(8,128)(2,1)}, bf16[1,2,512,128]{3,2,1,0:T(8,128)(2,1)}, u32[]{:S(2)}, u32[]{:S(2)}) collective-permute-start(bf16[1,2,512,128]{3,2,1,0:T(8,128)(2,1)} %get-tuple-element.52), channel_id=1, source_target_pairs={{1,8},{3,10},{5,12},{7,14},{9,16},{11,18},{13,20},{15,22},{17,24},... | collective-permute-start | bytes 786440 | tf_op jit(solution)/shard_map/ppermute | solution.py:516
  111.3 26.8 %all-to-all-start.2 = ((bf16[8,512,128]{2,1,0:T(8,128)(2,1)}), bf16[8,512,128]{2,1,0:T(8,128)(2,1)S(1)}, u32[]{:S(2)}, u32[]{:S(2)}) async-start(bf16[8,512,128]{2,1,0:T(8,128)(2,1)} %get-tuple-element.39), calls=%async_computation.2 | async-start | bytes 2097152 | tf_op jit(solution)/shard_map/all_to_all | solution.py:501
  118.3 13.8 %collective-permute-start.16 = (bf16[2,2,512,128]{3,2,1,0:T(8,128)(2,1)}, bf16[2,2,512,128]{3,2,1,0:T(8,128)(2,1)S(1)}, u32[]{:S(2)}, u32[]{:S(2)}) collective-permute-start(bf16[2,2,512,128]{3,2,1,0:T(8,128)(2,1)} %get-tuple-element.60), channel_id=1, source_target_pairs={{0,8},{2,10},{4,12},{6,14},{8,16},{10,18},{12,20},{14,22},{16,24},... | collective-permute-start | bytes 1572872 | tf_op jit(solution)/shard_map/ppermute | solution.py:509
  120.0 1.4 copy-start.17
  120.0 18.1 %collective-permute-start.17 = (bf16[2,2,512,128]{3,2,1,0:T(8,128)(2,1)}, bf16[2,2,512,128]{3,2,1,0:T(8,128)(2,1)S(1)}, u32[]{:S(2)}, u32[]{:S(2)}) collective-permute-start(bf16[2,2,512,128]{3,2,1,0:T(8,128)(2,1)} %get-tuple-element.61), channel_id=1, source_target_pairs={{8,0},{10,2},{12,4},{14,6},{16,8},{18,10},{20,12},{22,14},{24,16},... | collective-permute-start | bytes 1572872 | tf_op jit(solution)/shard_map/ppermute | solution.py:512
  126.2 19.1 %collective-permute-start.13 = (bf16[3,512,128]{2,1,0:T(8,128)(2,1)}, bf16[3,512,128]{2,1,0:T(8,128)(2,1)S(1)}, u32[]{:S(2)}, u32[]{:S(2)}) collective-permute-start(bf16[3,512,128]{2,1,0:T(8,128)(2,1)} %get-tuple-element.55), channel_id=1, source_target_pairs={{0,2},{2,0},{4,6},{6,4},{8,10},{10,8},{12,14},{14,12},{16,18},{18,... | collective-permute-start | bytes 1179656 | tf_op jit(solution)/shard_map/ppermute | solution.py:496
  128.2 17.1 %collective-permute-start.14 = (bf16[3,512,128]{2,1,0:T(8,128)(2,1)}, bf16[3,512,128]{2,1,0:T(8,128)(2,1)}, u32[]{:S(2)}, u32[]{:S(2)}) collective-permute-start(bf16[3,512,128]{2,1,0:T(8,128)(2,1)} %get-tuple-element.56), channel_id=1, source_target_pairs={{0,4},{2,6},{4,0},{6,2},{8,12},{10,14},{12,8},{14,10},{16,20},{18,... | collective-permute-start | bytes 1179656 | tf_op jit(solution)/shard_map/ppermute | solution.py:496
  129.7 21.5 %collective-permute-start.15 = (bf16[3,512,128]{2,1,0:T(8,128)(2,1)}, bf16[3,512,128]{2,1,0:T(8,128)(2,1)}, u32[]{:S(2)}, u32[]{:S(2)}) collective-permute-start(bf16[3,512,128]{2,1,0:T(8,128)(2,1)} %get-tuple-element.57), channel_id=1, source_target_pairs={{0,6},{2,4},{4,2},{6,0},{8,14},{10,12},{12,10},{14,8},{16,22},{18,... | collective-permute-start | bytes 1179656 | tf_op jit(solution)/shard_map/ppermute | solution.py:496
  138.1 1.6 copy-start.10
  141.3 9.9 %copy-start.9 = (s32[2]{0:T(128)S(1)}, s32[2]{0:T(128)}, u32[]{:S(2)}) copy-start(s32[2]{0:T(128)} %pad_add_fusion.place) | copy-start | bytes 28
  141.3 31.8 %all-to-all-start.3 = ((bf16[8,2,512,128]{3,2,1,0:T(8,128)(2,1)}), bf16[8,2,512,128]{3,2,1,0:T(8,128)(2,1)S(1)}, u32[]{:S(2)}, u32[]{:S(2)}) async-start(bf16[8,2,512,128]{3,2,1,0:T(8,128)(2,1)} %whole_settle.1), calls=%async_computation.3 | async-start | bytes 4194304 | tf_op jit(solution)/shard_map/all_to_all | solution.py:501
  (8 other events, 6.8 us)
where the time goes:
time: 177 us; the launch traced here: 175 us
  Pallas kernels  58 us (33%)
  waiting for transfers between devices  53.4 us (30%)
  starting transfers between devices  50.3 us (28%)
  local copies, waits for them, and re-layouts  11.3 us (6%)
    all_to_all x4, waiting for transfers between devices, regroup_wide(): lax.all_to_all(member, ('seq', 'head'), split_axis=0, concat_axis=0, axis...  24.8 us
    pallas_call x1, Pallas kernels, whole_grads(): pl.pallas_call(functools.partial(whole_grads_kernel, len(after)), out_sha...  23 us
    ppermute x6, waiting for transfers between devices, across(): lax.ppermute(members[away], 'seq', [(c, c ^ away) for c in range(chips)])  20.1 us
    all_to_all x4, starting transfers between devices, regroup_wide(): lax.all_to_all(member, ('seq', 'head'), split_axis=0, concat_axis=0, axis...  19.5 us
    ppermute x4, starting transfers between devices, upward(): lax.ppermute(member, 'seq', [(c, c + GROUP) for c in range(chips - GROUP)])  14.6 us
    pallas_call x1, Pallas kernels, split_grads(): pl.pallas_call(functools.partial(split_grads_kernel, len(after)), out_sha...  13.3 us
    unnamed x37, local copies, waits for them, and re-layouts  10.6 us
    ppermute x6, starting transfers between devices, across(): lax.ppermute(members[away], 'seq', [(c, c ^ away) for c in range(chips)])  8.03 us
  transfers between devices with their start and end apart: 22, of which 7 were waited for; matrix products, arithmetic and copies ran while one was open for 0% of the time, Pallas kernels for 30%

commit v1 on v0

--- a/solution.py
+++ b/solution.py
@@ -20,7 +20,7 @@
 MEMBERS = GROUP * CORES
 SCALE = HEAD_DIM ** -0.5
 LOG_SCALE = SCALE * math.log2(math.e)
-COST_FLOPS, COST_BYTES = 3.45e+09, 9.00e+06
+COST_FLOPS, COST_BYTES = 4.02e+09, 1.05e+07
 VMEM_LIMIT = 60 * 1024 * 1024
 
 ANYWHERE = pl.BlockSpec(memory_space=pl.ANY)
@@ -166,7 +166,9 @@
     )(place, member, *after)
 
 
-def grads_core(first, place_of, spots, block_of, keys, rows, sums, queries, lists, counts):
+def grads_core(
+    first, place_of, spots, block_of, keys, rows, sums, queries, lists, counts, after_spot=None
+):
     def query_step(spot, carry):
         block = block_of(spot)
         count = counts[block]
@@ -198,6 +200,8 @@
 
         for slots in range(1, MAXK + 1):
             pl.when(count == slots)(functools.partial(live, slots))
+        if after_spot is not None:
+            after_spot(spot)
         return carry
 
     lax.fori_loop(0, spots, query_step, 0)
@@ -310,28 +314,45 @@
     sums[...] = jnp.zeros_like(sums)
     for copy in copies:
         copy.wait()
+
+    def query_copy(spot):
+        return pltpu.make_async_copy(queries.at[spot], query_out.at[spot], sem.at[4 + spot])
+
+    def low_copy(spot):
+        return pltpu.make_async_copy(rounded.at[spot], low_out.at[spot], sem.at[12 + spot])
+
+    def sum_copy(spot):
+        return pltpu.make_async_copy(rounded.at[spot], sum_out.at[spot - 2], sem.at[12 + spot])
+
+    def after_spot(spot):
+        rounded[spot] = sums[spot].astype(jnp.bfloat16)
+        query_copy(spot).start()
+        pl.when(spot < 2)(lambda: low_copy(spot).start())
+        pl.when(spot >= 2)(lambda: sum_copy(spot).start())
+
     grads_core(
         first, lambda offset: offset, MEMBERS, lambda spot: first + 2 + spot,
-        keys, rows, sums, queries, lists, counts,
+        keys, rows, sums, queries, lists, counts, after_spot,
     )
     copies = begin(
         [
-            (queries, query_out),
             (sums.at[pl.ds(2, 2)], edge_out.at[pl.ds(0, 2)]),
             (sums.at[pl.ds(MEMBERS, 2)], edge_out.at[pl.ds(2, 2)]),
         ],
         sem,
     )
-    rounded[...] = sums[...].astype(jnp.bfloat16)
-    more = begin(
+    rounded[MEMBERS:] = sums[MEMBERS:].astype(jnp.bfloat16)
+    copies += begin(
         [
-            (rounded.at[pl.ds(2, MEMBERS)], sum_out),
-            (rounded.at[pl.ds(0, 2)], low_out),
+            (rounded.at[pl.ds(MEMBERS, 2)], sum_out.at[pl.ds(MEMBERS - 2, 2)]),
             (rounded.at[pl.ds(MEMBERS + 2, 2)], high_out),
         ],
-        sem.at[pl.ds(3, 3)],
-    )
-    for copy in copies + more:
+        sem.at[pl.ds(2, 2)],
+    )
+    for spot in range(MEMBERS):
+        copies.append(query_copy(spot))
+        copies.append(low_copy(spot) if spot < 2 else sum_copy(spot))
+    for copy in copies:
         copy.wait()
 
 
@@ -356,7 +377,7 @@
             pltpu.VMEM((MEMBERS + 4, 2) + block, jnp.float32),
             pltpu.VMEM((MEMBERS,) + block, jnp.bfloat16),
             pltpu.VMEM((MEMBERS + 4, 2) + block, jnp.bfloat16),
-            pltpu.SemaphoreType.DMA((6,)),
+            pltpu.SemaphoreType.DMA((2 * MEMBERS + 4,)),
         ],
         compiler_params=pltpu.CompilerParams(vmem_limit_bytes=VMEM_LIMIT),
         cost_estimate=cost(22),

time: 177 us -> 175 us (0.989); the launches traced: 175 us -> 176 us
  starting transfers between devices: 50.3 us -> 59.6 us
  Pallas kernels: 58 us -> 52.8 us
  waiting for transfers between devices: 53.4 us -> 50.2 us
    ppermute x4, starting transfers between devices: 14.6 us -> 20.2 us  [upward(): lax.ppermute(member, 'seq', [(c, c + GROUP) for c in range(chips - GROUP)])]
    ppermute x2, starting transfers between devices: 0.26 us -> 3.94 us  [swap(): return lax.ppermute(member, 'head', [(0, 1), (1, 0)])]
    pallas_call x1, Pallas kernels: 13.3 us -> 10.5 us  [split_grads(): pl.pallas_call(functools.partial(split_grads_kernel, len(after)), out_sha...]
    pallas_call x1, Pallas kernels: 23 us -> 20.5 us  [whole_grads(): pl.pallas_call(functools.partial(whole_grads_kernel, len(after)), out_sha...]
    ppermute x4, waiting for transfers between devices: 6 us -> 4.07 us  [downward(): lax.ppermute(member, 'seq', [(c + GROUP, c) for c in range(chips - GROUP)])]
  transfers between devices with their start and end apart: 22 -> 22, of which waited for: 7 -> 7; matrix products, arithmetic and copies ran while one was open for 0% -> 0% of each run, Pallas kernels for 30% -> 27%
where the time goes in v1:
time: 175 us; the launch traced here: 176 us
  starting transfers between devices  59.6 us (34%)
  Pallas kernels  52.8 us (30%)
  waiting for transfers between devices  50.2 us (29%)
  local copies, waits for them, and re-layouts  11.3 us (6%)
    all_to_all x4, waiting for transfers between devices, regroup_wide(): lax.all_to_all(member, ('seq', 'head'), split_axis=0, concat_axis=0, axis...  25.1 us
    pallas_call x1, Pallas kernels, whole_grads(): pl.pallas_call(functools.partial(whole_grads_kernel, len(after)), out_sha...  20.5 us
    ppermute x4, starting transfers between devices, upward(): lax.ppermute(member, 'seq', [(c, c + GROUP) for c in range(chips - GROUP)])  20.2 us
    all_to_all x4, starting transfers between devices, regroup_wide(): lax.all_to_all(member, ('seq', 'head'), split_axis=0, concat_axis=0, axis...  19.5 us
    ppermute x6, waiting for transfers between devices, across(): lax.ppermute(members[away], 'seq', [(c, c ^ away) for c in range(chips)])  18.6 us
    unnamed x37, local copies, waits for them, and re-layouts  10.6 us
    pallas_call x1, Pallas kernels, split_grads(): pl.pallas_call(functools.partial(split_grads_kernel, len(after)), out_sha...  10.5 us
    ppermute x6, starting transfers between devices, across(): lax.ppermute(members[away], 'seq', [(c, c ^ away) for c in range(chips)])  8.03 us
  transfers between devices with their start and end apart: 22, of which 7 were waited for; matrix products, arithmetic and copies ran while one was open for 0% of the time, Pallas kernels for 27%

profile of v1, /device:TPU:0, one launch (start us, length us, event | category | flops | bytes accessed | tf_op | source)
XLA Modules:
  0.0 175.6 jit_solution(15195850271941672416)
XLA Ops:
  1.3 3.8 %pack_split.1 = (bf16[4,512,128]{2,1,0:T(8,128)(2,1)}, bf16[4,512,128]{2,1,0:T(8,128)(2,1)}, bf16[4,512,128]{2,1,0:T(8,128)(2,1)}, bf16[4,512,128]{2,1,0:T(8,128)(2,1)}) custom-call(s32[2]{0:T(128)} %pad_add_fusion.place, bf16[512,1536]{1,0:T(8,128)(2,1)} %key_rows.1, bf16[512,1536]{1,0:T(8,128)(2,1)} %value_rows.1, bf16[512,1536]{1,0:T(8,128)(2,1)} %query_rows.1, ...), custom_call_target="tpu_custom_call" | custom-call | flops 16080000000 | bytes 42000000 | tf_op jit(solution)/shard_map/pack_split/pallas_call | solution.py:78
  5.1 3.0 %collective-permute-start.2 = (bf16[4,512,128]{2,1,0:T(8,128)(2,1)}, bf16[4,512,128]{2,1,0:T(8,128)(2,1)S(1)}, u32[]{:S(2)}, u32[]{:S(2)}) collective-permute-start(bf16[4,512,128]{2,1,0:T(8,128)(2,1)} %get-tuple-element.41), channel_id=1, source_target_pairs={{0,2},{2,0},{4,6},{6,4},{8,10},{10,8},{12,14},{14,12},{16,18},{18,... | collective-permute-start | bytes 1572872 | tf_op jit(solution)/shard_map/ppermute | solution.py:517
  8.1 1.5 collective-permute-start.3
  9.6 4.7 %pack.1 = (bf16[8,2,512,128]{3,2,1,0:T(8,128)(2,1)}, bf16[8,2,512,128]{3,2,1,0:T(8,128)(2,1)}) custom-call(bf16[512,1536]{1,0:T(8,128)(2,1)} %key_rows.1, bf16[512,1536]{1,0:T(8,128)(2,1)} %value_rows.1, bf16[512,1536]{1,0:T(8,128)(2,1)} %query_rows.1, bf16[512,1536]{1,0:T(8,128)(2,1)} %out_grad.1), custom_call_target="tpu_custom_call" | custom-call | flops 24120000512 | bytes 63000000 | tf_op jit(solution)/shard_map/pack/pallas_call | solution.py:102
  14.3 4.2 %all-to-all-start = ((bf16[8,2,512,128]{3,2,1,0:T(8,128)(2,1)}), bf16[8,2,512,128]{3,2,1,0:T(8,128)(2,1)S(1)}, u32[]{:S(2)}, u32[]{:S(2)}) async-start(bf16[8,2,512,128]{3,2,1,0:T(8,128)(2,1)} %get-tuple-element.35), calls=%async_computation | async-start | bytes 4194304 | tf_op jit(solution)/shard_map/all_to_all | solution.py:522
  18.5 2.6 %collective-permute-done.2.refs_1_.refs_6_ = bf16[4,512,128]{2,1,0:T(8,128)(2,1)S(1)} collective-permute-done((bf16[4,512,128]{2,1,0:T(8,128)(2,1)}, bf16[4,512,128]{2,1,0:T(8,128)(2,1)S(1)}, u32[]{:S(2)}, u32[]{:S(2)}) %collective-permute-start.2) | collective-permute-done | bytes 524320 | tf_op jit(solution)/shard_map/ppermute | solution.py:517
  21.8 11.7 %collective-permute-done.3.refs_2_.refs_7_ = bf16[4,512,128]{2,1,0:T(8,128)(2,1)S(1)} collective-permute-done((bf16[4,512,128]{2,1,0:T(8,128)(2,1)}, bf16[4,512,128]{2,1,0:T(8,128)(2,1)S(1)}, u32[]{:S(2)}, u32[]{:S(2)}) %collective-permute-start.3) | collective-permute-done | bytes 524320 | tf_op jit(solution)/shard_map/ppermute | solution.py:517
  37.5 1.6 arrange.1
  41.3 4.2 %collective-permute-start.6 = (bf16[1,2,512,128]{3,2,1,0:T(8,128)(2,1)}, bf16[1,2,512,128]{3,2,1,0:T(8,128)(2,1)}, u32[]{:S(2)}, u32[]{:S(2)}) collective-permute-start(bf16[1,2,512,128]{3,2,1,0:T(8,128)(2,1)} %copy-done.7), channel_id=1, source_target_pairs={{0,8},{2,10},{4,12},{6,14},{8,16},{10,18},{12,20},{14,22},{16,24},... | collective-permute-start | bytes 786440 | tf_op jit(solution)/shard_map/ppermute | solution.py:530
  48.2 7.2 %all-to-all-done.member.refs_0_ = bf16[8,2,512,128]{3,2,1,0:T(8,128)(2,1)S(1)} async-done(((bf16[8,2,512,128]{3,2,1,0:T(8,128)(2,1)}), bf16[8,2,512,128]{3,2,1,0:T(8,128)(2,1)S(1)}, u32[]{:S(2)}, u32[]{:S(2)}) %all-to-all-start) | async-done | bytes 2097184 | tf_op jit(solution)/shard_map/all_to_all | solution.py:522
  55.4 4.4 %all-to-all-start.1 = ((bf16[8,2,512,128]{3,2,1,0:T(8,128)(2,1)}), bf16[8,2,512,128]{3,2,1,0:T(8,128)(2,1)}, u32[]{:S(2)}, u32[]{:S(2)}) async-start(bf16[8,2,512,128]{3,2,1,0:T(8,128)(2,1)} %get-tuple-element.38), calls=%async_computation.1 | async-start | bytes 4194304 | tf_op jit(solution)/shard_map/all_to_all | solution.py:522
  59.8 1.4 cut.1
  61.2 3.5 %collective-permute-start = (bf16[2,2,512,128]{3,2,1,0:T(8,128)(2,1)S(1)}, bf16[2,2,512,128]{3,2,1,0:T(8,128)(2,1)S(1)}, u32[]{:S(2)}, u32[]{:S(2)}) collective-permute-start(bf16[2,2,512,128]{3,2,1,0:T(8,128)(2,1)S(1)} %get-tuple-element.36), channel_id=1, source_target_pairs={{0,8},{2,10},{4,12},{6,14},{8,16},{10,18},{12,20},{14,22},{16,24},... | collective-permute-start | bytes 1572872 | tf_op jit(solution)/shard_map/ppermute | solution.py:530
  66.1 10.5 %split_grads.1 = (bf16[4,512,128]{2,1,0:T(8,128)(2,1)}, f32[4,2,512,128]{3,2,1,0:T(8,128)}, bf16[4,2,512,128]{3,2,1,0:T(8,128)(2,1)}, bf16[1,2,512,128]{3,2,1,0:...) custom-call(s32[2]{0:T(128)} %pad_add_fusion.place, s32[96]{0:T(128)} %reshape.9.lists, ...), custom_call_target="tpu_custom_call" | custom-call | flops 52259999744 | bytes 136500000 | tf_op jit(solution)/shard_map/split_grads/pallas_call | solution.py:280
  76.6 3.9 %collective-permute-start.9 = (bf16[4,2,512,128]{3,2,1,0:T(8,128)(2,1)}, bf16[4,2,512,128]{3,2,1,0:T(8,128)(2,1)S(1)}, u32[]{:S(2)}, u32[]{:S(2)}) collective-permute-start(bf16[4,2,512,128]{3,2,1,0:T(8,128)(2,1)} %get-tuple-element.49), channel_id=1, source_target_pairs={{0,1},{1,0},{2,3},{3,2},{4,5},{5,4},{6,7},{7,6},{8,9},{9,8},{10,11... | collective-permute-start | bytes 3145736 | tf_op jit(solution)/shard_map/ppermute | solution.py:527
  80.6 5.2 %collective-permute-start.10 = (bf16[1,2,512,128]{3,2,1,0:T(8,128)(2,1)}, bf16[1,2,512,128]{3,2,1,0:T(8,128)(2,1)S(1)}, u32[]{:S(2)}, u32[]{:S(2)}) collective-permute-start(bf16[1,2,512,128]{3,2,1,0:T(8,128)(2,1)} %get-tuple-element.50), channel_id=1, source_target_pairs={{0,8},{2,10},{4,12},{6,14},{8,16},{10,18},{12,20},{14,22},{16,24},... | collective-permute-start | bytes 786440 | tf_op jit(solution)/shard_map/ppermute | solution.py:530
  87.1 1.4 collective-permute-start.12
  89.3 20.5 %whole_grads.1 = (bf16[8,512,128]{2,1,0:T(8,128)(2,1)}, bf16[8,2,512,128]{3,2,1,0:T(8,128)(2,1)}, f32[4,2,512,128]{3,2,1,0:T(8,128)}, bf16[2,2,512,128]{3,2,1,0:T(8,128)(2,1)}, bf16[2,2,512,128]{3,2,1,0:T(8,128)(2,1)}) custom-call(s32[2]{0:T(128)} %pad_add_fusion.place, s32[96]{0:T(128)} %reshape.9.lists, s32[32]{0:T(128)} %counts.3, ...), custom_call_target="tpu_custom_call" | custom-call | flops 88439996416 | bytes 231000000 | tf_op jit(solution)/shard_map/whole_grads/pallas_call | solution.py:369
  109.8 7.0 %all-to-all-start.2 = ((bf16[8,512,128]{2,1,0:T(8,128)(2,1)}), bf16[8,512,128]{2,1,0:T(8,128)(2,1)S(1)}, u32[]{:S(2)}, u32[]{:S(2)}) async-start(bf16[8,512,128]{2,1,0:T(8,128)(2,1)} %get-tuple-element.39), calls=%async_computation.2 | async-start | bytes 2097152 | tf_op jit(solution)/shard_map/all_to_all | solution.py:522
  116.8 7.3 %collective-permute-start.16 = (bf16[2,2,512,128]{3,2,1,0:T(8,128)(2,1)}, bf16[2,2,512,128]{3,2,1,0:T(8,128)(2,1)S(1)}, u32[]{:S(2)}, u32[]{:S(2)}) collective-permute-start(bf16[2,2,512,128]{3,2,1,0:T(8,128)(2,1)} %get-tuple-element.60), channel_id=1, source_target_pairs={{0,8},{2,10},{4,12},{6,14},{8,16},{10,18},{12,20},{14,22},{16,24},... | collective-permute-start | bytes 1572872 | tf_op jit(solution)/shard_map/ppermute | solution.py:530
  126.4 3.8 %split_settle.1 = (bf16[3,512,128]{2,1,0:T(8,128)(2,1)}, bf16[3,512,128]{2,1,0:T(8,128)(2,1)}, bf16[3,512,128]{2,1,0:T(8,128)(2,1)}, bf16[3,512,128]{2,1,0:T(8,128)(2,1)}) custom-call(s32[2]{0:T(128)} %pad_add_fusion.place, f32[4,2,512,128]{3,2,1,0:T(8,128)} %get-tuple-element.48.near, bf16[4,2,512,128]{3,2,1,0:T(8,128)(2,1)} %copy-done.14, ...), custom_call_target="tpu_custom_call" | custom-call | flops 16080000000 | bytes 42000000 | tf_op jit(solution)/shard_map/split_settle/pallas_call | solution.py:411
  130.2 2.0 %collective-permute-start.13 = (bf16[3,512,128]{2,1,0:T(8,128)(2,1)}, bf16[3,512,128]{2,1,0:T(8,128)(2,1)S(1)}, u32[]{:S(2)}, u32[]{:S(2)}) collective-permute-start(bf16[3,512,128]{2,1,0:T(8,128)(2,1)} %get-tuple-element.55), channel_id=1, source_target_pairs={{0,2},{2,0},{4,6},{6,4},{8,10},{10,8},{12,14},{14,12},{16,18},{18,... | collective-permute-start | bytes 1179656 | tf_op jit(solution)/shard_map/ppermute | solution.py:517
  132.2 1.5 collective-permute-start.14
  133.7 2.5 %collective-permute-done.16.below = bf16[2,2,512,128]{3,2,1,0:T(8,128)(2,1)S(1)} collective-permute-done((bf16[2,2,512,128]{3,2,1,0:T(8,128)(2,1)}, bf16[2,2,512,128]{3,2,1,0:T(8,128)(2,1)S(1)}, u32[]{:S(2)}, u32[]{:S(2)}) %collective-permute-start.16) | collective-permute-done | bytes 524320 | tf_op jit(solution)/shard_map/ppermute | solution.py:530
  136.2 4.1 %collective-permute-done.17.above = bf16[2,2,512,128]{3,2,1,0:T(8,128)(2,1)S(1)} collective-permute-done((bf16[2,2,512,128]{3,2,1,0:T(8,128)(2,1)}, bf16[2,2,512,128]{3,2,1,0:T(8,128)(2,1)S(1)}, u32[]{:S(2)}, u32[]{:S(2)}) %collective-permute-start.17) | collective-permute-done | bytes 524320 | tf_op jit(solution)/shard_map/ppermute | solution.py:533
  140.2 1.6 copy-done.10
  141.8 1.6 whole_settle.1
  143.4 4.0 %all-to-all-start.3 = ((bf16[8,2,512,128]{3,2,1,0:T(8,128)(2,1)}), bf16[8,2,512,128]{3,2,1,0:T(8,128)(2,1)S(1)}, u32[]{:S(2)}, u32[]{:S(2)}) async-start(bf16[8,2,512,128]{3,2,1,0:T(8,128)(2,1)} %whole_settle.1), calls=%async_computation.3 | async-start | bytes 4194304 | tf_op jit(solution)/shard_map/all_to_all | solution.py:522
  147.4 4.4 %collective-permute-done.14.refs_2_ = bf16[3,512,128]{2,1,0:T(8,128)(2,1)} collective-permute-done((bf16[3,512,128]{2,1,0:T(8,128)(2,1)}, bf16[3,512,128]{2,1,0:T(8,128)(2,1)}, u32[]{:S(2)}, u32[]{:S(2)}) %collective-permute-start.14) | collective-permute-done | bytes 393248 | tf_op jit(solution)/shard_map/ppermute | solution.py:517
  152.8 2.4 %gather_split.1 = (bf16[512,1536]{1,0:T(8,128)(2,1)}, bf16[512,1536]{1,0:T(8,128)(2,1)}, bf16[512,1536]{1,0:T(8,128)(2,1)}) custom-call(s32[2]{0:T(128)S(1)} %copy-done.9, bf16[3,512,128]{2,1,0:T(8,128)(2,1)S(1)} %copy-done.12, bf16[3,512,128]{2,1,0:T(8,128)(2,1)S(1)} %collective-permute-done.13.refs_1_, ...), custom_call_target="tpu_custom_call" | custom-call | flops 12060000256 | bytes 31500000 | tf_op jit(solution)/shard_map/gather_split/pallas_call | solution.py:470
  156.2 17.8 %all-to-all-done.3.refs_0_ = bf16[8,2,512,128]{3,2,1,0:T(8,128)(2,1)S(1)} async-done(((bf16[8,2,512,128]{3,2,1,0:T(8,128)(2,1)}), bf16[8,2,512,128]{3,2,1,0:T(8,128)(2,1)S(1)}, u32[]{:S(2)}, u32[]{:S(2)}) %all-to-all-start.3) | async-done | bytes 2097184 | tf_op jit(solution)/shard_map/all_to_all | solution.py:522
  174.0 1.4 gather.3
  (62 shorter events, 17.9 us)
Async XLA Ops:
  5.1 16.0 %collective-permute-start.2 = (bf16[4,512,128]{2,1,0:T(8,128)(2,1)}, bf16[4,512,128]{2,1,0:T(8,128)(2,1)S(1)}, u32[]{:S(2)}, u32[]{:S(2)}) collective-permute-start(bf16[4,512,128]{2,1,0:T(8,128)(2,1)} %get-tuple-element.41), channel_id=1, source_target_pairs={{0,2},{2,0},{4,6},{6,4},{8,10},{10,8},{12,14},{14,12},{16,18},{18,... | collective-permute-start | bytes 1572872 | tf_op jit(solution)/shard_map/ppermute | solution.py:517
  8.1 25.4 %collective-permute-start.3 = (bf16[4,512,128]{2,1,0:T(8,128)(2,1)}, bf16[4,512,128]{2,1,0:T(8,128)(2,1)S(1)}, u32[]{:S(2)}, u32[]{:S(2)}) collective-permute-start(bf16[4,512,128]{2,1,0:T(8,128)(2,1)} %get-tuple-element.42), channel_id=1, source_target_pairs={{0,4},{2,6},{4,0},{6,2},{8,12},{10,14},{12,8},{14,10},{16,20},{18,... | collective-permute-start | bytes 1572872 | tf_op jit(solution)/shard_map/ppermute | solution.py:517
  9.6 24.7 %collective-permute-start.4 = (bf16[4,512,128]{2,1,0:T(8,128)(2,1)}, bf16[4,512,128]{2,1,0:T(8,128)(2,1)}, u32[]{:S(2)}, u32[]{:S(2)}) collective-permute-start(bf16[4,512,128]{2,1,0:T(8,128)(2,1)} %get-tuple-element.43), channel_id=1, source_target_pairs={{0,6},{2,4},{4,2},{6,0},{8,14},{10,12},{12,10},{14,8},{16,22},{18,... | collective-permute-start | bytes 1572872 | tf_op jit(solution)/shard_map/ppermute | solution.py:517
  14.3 20.1 %copy-start.8 = (s32[2]{0:T(128)S(1)}, s32[2]{0:T(128)}, u32[]{:S(2)}) copy-start(s32[2]{0:T(128)} %pad_add_fusion.place) | copy-start | bytes 28
  14.3 41.1 %all-to-all-start = ((bf16[8,2,512,128]{3,2,1,0:T(8,128)(2,1)}), bf16[8,2,512,128]{3,2,1,0:T(8,128)(2,1)S(1)}, u32[]{:S(2)}, u32[]{:S(2)}) async-start(bf16[8,2,512,128]{3,2,1,0:T(8,128)(2,1)} %get-tuple-element.35), calls=%async_computation | async-start | bytes 4194304 | tf_op jit(solution)/shard_map/all_to_all | solution.py:522
  34.3 1.0 copy-start.3
  35.4 1.0 copy-start.5
  37.5 3.1 %copy-start.13 = (s32[32,3]{0,1:T(4,128)S(1)}, s32[32,3]{0,1:T(4,128)}, u32[]{:S(2)}) copy-start(s32[32,3]{0,1:T(4,128)} %param.10) | copy-start | bytes 1156
  39.8 15.6 %copy-start.1 = (bf16[4,2,512,128]{3,2,1,0:T(8,128)(2,1)}, bf16[4,2,512,128]{3,2,1,0:T(8,128)(2,1)S(1)}, u32[]{:S(2)}) copy-start(bf16[4,2,512,128]{3,2,1,0:T(8,128)(2,1)S(1)} %get-tuple-element.44.refs_0_) | copy-start | bytes 3145732
  40.5 25.6 %collective-permute-start.5 = (bf16[4,2,512,128]{3,2,1,0:T(8,128)(2,1)S(1)}, bf16[4,2,512,128]{3,2,1,0:T(8,128)(2,1)}, u32[]{:S(2)}, u32[]{:S(2)}) collective-permute-start(bf16[4,2,512,128]{3,2,1,0:T(8,128)(2,1)S(1)} %get-tuple-element.44.refs_0_), channel_id=1, source_target_pairs={{0,1},{1,0},{2,3},{3,2},{4,5},{5,4},{6,7},{7,6},{8,9},{9,8},{10,11... | collective-permute-start | bytes 3145736 | tf_op jit(solution)/shard_map/ppermute | solution.py:527
  41.3 23.4 %collective-permute-start.6 = (bf16[1,2,512,128]{3,2,1,0:T(8,128)(2,1)}, bf16[1,2,512,128]{3,2,1,0:T(8,128)(2,1)}, u32[]{:S(2)}, u32[]{:S(2)}) collective-permute-start(bf16[1,2,512,128]{3,2,1,0:T(8,128)(2,1)} %copy-done.7), channel_id=1, source_target_pairs={{0,8},{2,10},{4,12},{6,14},{8,16},{10,18},{12,20},{14,22},{16,24},... | collective-permute-start | bytes 786440 | tf_op jit(solution)/shard_map/ppermute | solution.py:530
  45.5 20.5 %collective-permute-start.7 = (bf16[1,2,512,128]{3,2,1,0:T(8,128)(2,1)}, bf16[1,2,512,128]{3,2,1,0:T(8,128)(2,1)}, u32[]{:S(2)}, u32[]{:S(2)}) collective-permute-start(bf16[1,2,512,128]{3,2,1,0:T(8,128)(2,1)} %copy-done.6), channel_id=1, source_target_pairs={{8,0},{10,2},{12,4},{14,6},{16,8},{18,10},{20,12},{22,14},{24,16},... | collective-permute-start | bytes 786440 | tf_op jit(solution)/shard_map/ppermute | solution.py:533
  46.8 19.3 %collective-permute-start.8 = (bf16[1,2,512,128]{3,2,1,0:T(8,128)(2,1)S(1)}, bf16[1,2,512,128]{3,2,1,0:T(8,128)(2,1)}, u32[]{:S(2)}, u32[]{:S(2)}) collective-permute-start(bf16[1,2,512,128]{3,2,1,0:T(8,128)(2,1)S(1)} %get-tuple-element.47), channel_id=1, source_target_pairs={{1,8},{3,10},{5,12},{7,14},{9,16},{11,18},{13,20},{15,22},{17,24},... | collective-permute-start | bytes 786440 | tf_op jit(solution)/shard_map/ppermute | solution.py:537
  55.4 4.4 %copy-start = (bf16[8,2,512,128]{3,2,1,0:T(8,128)(2,1)}, bf16[8,2,512,128]{3,2,1,0:T(8,128)(2,1)S(1)}, u32[]{:S(2)}) copy-start(bf16[8,2,512,128]{3,2,1,0:T(8,128)(2,1)S(1)} %all-to-all-done.member.refs_0_) | copy-start | bytes 6291460
  55.4 33.1 %all-to-all-start.1 = ((bf16[8,2,512,128]{3,2,1,0:T(8,128)(2,1)}), bf16[8,2,512,128]{3,2,1,0:T(8,128)(2,1)}, u32[]{:S(2)}, u32[]{:S(2)}) async-start(bf16[8,2,512,128]{3,2,1,0:T(8,128)(2,1)} %get-tuple-element.38), calls=%async_computation.1 | async-start | bytes 4194304 | tf_op jit(solution)/shard_map/all_to_all | solution.py:522
  61.2 25.9 %collective-permute-start = (bf16[2,2,512,128]{3,2,1,0:T(8,128)(2,1)S(1)}, bf16[2,2,512,128]{3,2,1,0:T(8,128)(2,1)S(1)}, u32[]{:S(2)}, u32[]{:S(2)}) collective-permute-start(bf16[2,2,512,128]{3,2,1,0:T(8,128)(2,1)S(1)} %get-tuple-element.36), channel_id=1, source_target_pairs={{0,8},{2,10},{4,12},{6,14},{8,16},{10,18},{12,20},{14,22},{16,24},... | collective-permute-start | bytes 1572872 | tf_op jit(solution)/shard_map/ppermute | solution.py:530
  64.7 23.7 %collective-permute-start.1 = (bf16[2,2,512,128]{3,2,1,0:T(8,128)(2,1)}, bf16[2,2,512,128]{3,2,1,0:T(8,128)(2,1)S(1)}, u32[]{:S(2)}, u32[]{:S(2)}) collective-permute-start(bf16[2,2,512,128]{3,2,1,0:T(8,128)(2,1)} %get-tuple-element.37), channel_id=1, source_target_pairs={{8,0},{10,2},{12,4},{14,6},{16,8},{18,10},{20,12},{22,14},{24,16},... | collective-permute-start | bytes 1572872 | tf_op jit(solution)/shard_map/ppermute | solution.py:533
  76.6 48.8 %collective-permute-start.9 = (bf16[4,2,512,128]{3,2,1,0:T(8,128)(2,1)}, bf16[4,2,512,128]{3,2,1,0:T(8,128)(2,1)S(1)}, u32[]{:S(2)}, u32[]{:S(2)}) collective-permute-start(bf16[4,2,512,128]{3,2,1,0:T(8,128)(2,1)} %get-tuple-element.49), channel_id=1, source_target_pairs={{0,1},{1,0},{2,3},{3,2},{4,5},{5,4},{6,7},{7,6},{8,9},{9,8},{10,11... | collective-permute-start | bytes 3145736 | tf_op jit(solution)/shard_map/ppermute | solution.py:527
  80.6 43.5 %collective-permute-start.10 = (bf16[1,2,512,128]{3,2,1,0:T(8,128)(2,1)}, bf16[1,2,512,128]{3,2,1,0:T(8,128)(2,1)S(1)}, u32[]{:S(2)}, u32[]{:S(2)}) collective-permute-start(bf16[1,2,512,128]{3,2,1,0:T(8,128)(2,1)} %get-tuple-element.50), channel_id=1, source_target_pairs={{0,8},{2,10},{4,12},{6,14},{8,16},{10,18},{12,20},{14,22},{16,24},... | collective-permute-start | bytes 786440 | tf_op jit(solution)/shard_map/ppermute | solution.py:530
  85.8 39.6 %collective-permute-start.11 = (bf16[1,2,512,128]{3,2,1,0:T(8,128)(2,1)}, bf16[1,2,512,128]{3,2,1,0:T(8,128)(2,1)}, u32[]{:S(2)}, u32[]{:S(2)}) collective-permute-start(bf16[1,2,512,128]{3,2,1,0:T(8,128)(2,1)} %get-tuple-element.51), channel_id=1, source_target_pairs={{8,0},{10,2},{12,4},{14,6},{16,8},{18,10},{20,12},{22,14},{24,16},... | collective-permute-start | bytes 786440 | tf_op jit(solution)/shard_map/ppermute | solution.py:533
  87.1 1.4 copy-start.15
  87.1 38.3 %collective-permute-start.12 = (bf16[1,2,512,128]{3,2,1,0:T(8,128)(2,1)}, bf16[1,2,512,128]{3,2,1,0:T(8,128)(2,1)}, u32[]{:S(2)}, u32[]{:S(2)}) collective-permute-start(bf16[1,2,512,128]{3,2,1,0:T(8,128)(2,1)} %get-tuple-element.52), channel_id=1, source_target_pairs={{1,8},{3,10},{5,12},{7,14},{9,16},{11,18},{13,20},{15,22},{17,24},... | collective-permute-start | bytes 786440 | tf_op jit(solution)/shard_map/ppermute | solution.py:537
  109.8 30.5 %all-to-all-start.2 = ((bf16[8,512,128]{2,1,0:T(8,128)(2,1)}), bf16[8,512,128]{2,1,0:T(8,128)(2,1)S(1)}, u32[]{:S(2)}, u32[]{:S(2)}) async-start(bf16[8,512,128]{2,1,0:T(8,128)(2,1)} %get-tuple-element.39), calls=%async_computation.2 | async-start | bytes 2097152 | tf_op jit(solution)/shard_map/all_to_all | solution.py:522
  116.8 19.4 %collective-permute-start.16 = (bf16[2,2,512,128]{3,2,1,0:T(8,128)(2,1)}, bf16[2,2,512,128]{3,2,1,0:T(8,128)(2,1)S(1)}, u32[]{:S(2)}, u32[]{:S(2)}) collective-permute-start(bf16[2,2,512,128]{3,2,1,0:T(8,128)(2,1)} %get-tuple-element.60), channel_id=1, source_target_pairs={{0,8},{2,10},{4,12},{6,14},{8,16},{10,18},{12,20},{14,22},{16,24},... | collective-permute-start | bytes 1572872 | tf_op jit(solution)/shard_map/ppermute | solution.py:530
  124.1 1.4 copy-start.17
  124.1 16.2 %collective-permute-start.17 = (bf16[2,2,512,128]{3,2,1,0:T(8,128)(2,1)}, bf16[2,2,512,128]{3,2,1,0:T(8,128)(2,1)S(1)}, u32[]{:S(2)}, u32[]{:S(2)}) collective-permute-start(bf16[2,2,512,128]{3,2,1,0:T(8,128)(2,1)} %get-tuple-element.61), channel_id=1, source_target_pairs={{8,0},{10,2},{12,4},{14,6},{16,8},{18,10},{20,12},{22,14},{24,16},... | collective-permute-start | bytes 1572872 | tf_op jit(solution)/shard_map/ppermute | solution.py:533
  130.2 17.2 %collective-permute-start.13 = (bf16[3,512,128]{2,1,0:T(8,128)(2,1)}, bf16[3,512,128]{2,1,0:T(8,128)(2,1)S(1)}, u32[]{:S(2)}, u32[]{:S(2)}) collective-permute-start(bf16[3,512,128]{2,1,0:T(8,128)(2,1)} %get-tuple-element.55), channel_id=1, source_target_pairs={{0,2},{2,0},{4,6},{6,4},{8,10},{10,8},{12,14},{14,12},{16,18},{18,... | collective-permute-start | bytes 1179656 | tf_op jit(solution)/shard_map/ppermute | solution.py:517
  132.2 19.6 %collective-permute-start.14 = (bf16[3,512,128]{2,1,0:T(8,128)(2,1)}, bf16[3,512,128]{2,1,0:T(8,128)(2,1)}, u32[]{:S(2)}, u32[]{:S(2)}) collective-permute-start(bf16[3,512,128]{2,1,0:T(8,128)(2,1)} %get-tuple-element.56), channel_id=1, source_target_pairs={{0,4},{2,6},{4,0},{6,2},{8,12},{10,14},{12,8},{14,10},{16,20},{18,... | collective-permute-start | bytes 1179656 | tf_op jit(solution)/shard_map/ppermute | solution.py:517
  133.7 18.1 %collective-permute-start.15 = (bf16[3,512,128]{2,1,0:T(8,128)(2,1)}, bf16[3,512,128]{2,1,0:T(8,128)(2,1)}, u32[]{:S(2)}, u32[]{:S(2)}) collective-permute-start(bf16[3,512,128]{2,1,0:T(8,128)(2,1)} %get-tuple-element.57), channel_id=1, source_target_pairs={{0,6},{2,4},{4,2},{6,0},{8,14},{10,12},{12,10},{14,8},{16,22},{18,... | collective-permute-start | bytes 1179656 | tf_op jit(solution)/shard_map/ppermute | solution.py:517
  140.2 1.6 copy-start.10
  143.4 8.4 %copy-start.9 = (s32[2]{0:T(128)S(1)}, s32[2]{0:T(128)}, u32[]{:S(2)}) copy-start(s32[2]{0:T(128)} %pad_add_fusion.place) | copy-start | bytes 28
  143.4 30.6 %all-to-all-start.3 = ((bf16[8,2,512,128]{3,2,1,0:T(8,128)(2,1)}), bf16[8,2,512,128]{3,2,1,0:T(8,128)(2,1)S(1)}, u32[]{:S(2)}, u32[]{:S(2)}) async-start(bf16[8,2,512,128]{3,2,1,0:T(8,128)(2,1)} %whole_settle.1), calls=%async_computation.3 | async-start | bytes 4194304 | tf_op jit(solution)/shard_map/all_to_all | solution.py:522
  (8 other events, 6.8 us)
